TPU v7x, 32 devices: a whole 2x2x4 slice. The times are simulated.
32 devices in a mesh: dom: 8 (over z, core), sub: 4 (over y, x).
Axes of the slice: x: 2, y: 2, z: 4, core: 2. Of those that a mesh axis runs over, the one named last changes fastest.
Arguments:
- modal_state: float32 [56, 9, 4096], P(None, None, ('dom', 'sub')), may hold values from -6 to 6
- stiffness: float32 [3, 56, 56], replicated, may hold values from -0.75 to 0.75
- jacobians: float32 [3, 9, 9, 4096], P(None, None, None, ('dom', 'sub')), may hold values from -1.25 to 1.25
- flux_solvers: float32 [2, 4, 9, 9, 4096], P(None, None, None, None, ('dom', 'sub')), may hold values from -0.75 to 0.75
- projector: float32 [4, 21, 56], replicated, may hold values from -0.75 to 0.75
- rotations: float32 [3, 21, 21], replicated, may hold values from -1.25 to 1.25
- yield_stress: float32 [4096], P(('dom', 'sub')), may hold values from 0.5 to 8
- cluster: int32 [4096], P(('dom', 'sub')), may hold values from 0 to 1
- orient: int32 [4, 4096], P(None, ('dom', 'sub')), may hold values from 0 to 2
- neighbour_slot: int32 [4, 4096], P(None, ('dom', 'sub')), may hold values from 0 to 703, as said below
- send_map: int32 [6144], P(('dom', 'sub')), may hold values from 0 to 511, as said below
Outputs:
- updated: float32 [56, 9, 4096], P(None, None, ('dom', 'sub'))
Inputs may be any that keep to these rules, and one draw needn't show every extreme that they name: `neighbour_slot`: within one partition every received slot 512 + r is named by exactly one face; the other faces name local faces. `send_map`: the 192 entries of one partition are distinct local face numbers.
All inputs are finite; a program needn't handle non-finite values.
Results may differ from a plain program's by a relative error of at most 0.0003.
Values sent between devices are 32-bit elements; how exact they have to be, the bound alone decides.
No kernel may reach another device: no remote copies, remote signals or barrier semaphores. Data moves between devices by JAX's collectives and lax.ppermute only.
A program may use at most 64 MiB of HBM per device.

v0:
```python
import math

import jax
import jax.numpy as jnp
from jax import lax
from jax.experimental import pallas as pl
from jax.experimental.pallas import tpu as pltpu
from jax.sharding import PartitionSpec as P

ORDER = 6
SLOTS_DOM = 64
SLOTS_SUB = 32
ROWS = 24
GROUP = 3

F32 = jnp.float32
BF16 = jnp.bfloat16
EXACT = lax.Precision.HIGHEST

PACKING = (2, 2, 4, 4)

INPUTS = 11
FIRST_USED = 5


def iota(shape, dim):
    return lax.broadcasted_iota(jnp.int32, shape, dim)


def dot(a, b):
    return jnp.dot(a, b, preferred_element_type=F32)


def exact_dot(a, b):
    return jnp.dot(a, b, precision=EXACT, preferred_element_type=F32)


def halves(value):
    high = value.astype(BF16)
    return high, (value - high.astype(F32)).astype(BF16)


def one_hot(index_row, first, count, modulus=None):
    number = iota((count, index_row.shape[1]), 0)
    if modulus is not None:
        number = lax.rem(number, modulus)
    return jnp.where(number + first == index_row, 1.0, 0.0).astype(BF16)


def stack_rows(value):
    high = value.astype(BF16).astype(F32)
    return jnp.concatenate([high, value - high], axis=0).astype(BF16)


def gather(table, chosen):
    rows = table.shape[0]
    both = dot(stack_rows(table), chosen)
    return both[0:rows] + both[rows:2 * rows]


def fold_step(basis):
    return -(-basis // 16) * 16


def fold_rows(value):
    basis, lanes = value.shape
    rest = jnp.zeros((fold_step(basis) - basis, lanes), F32)
    value = jnp.concatenate([value, rest], axis=0)
    high, low = halves(value)
    return jnp.concatenate([high, high, low], axis=0)


def fold_columns(matrix):
    basis = matrix.shape[1]
    step = fold_step(basis)
    high, low = halves(matrix)
    row, column = iota((basis, 3 * step), 0), iota((basis, 3 * step), 1)
    outer = jnp.where((column == row) | (column == row + 2 * step), 1.0, 0.0).astype(BF16)
    inner = jnp.where(column == row + step, 1.0, 0.0).astype(BF16)
    return (dot(high, outer) + dot(low, inner)).astype(BF16)


def stiffen(stiff_fold, values, target, start, lanes):
    folded = jnp.concatenate([fold_rows(value) for value in values], axis=1)
    target[:, start * lanes:(start + len(values)) * lanes] = dot(stiff_fold, folded)


def mix_jacobians(stiffened, jac, basis, quants, lanes, take):
    for start in range(0, quants, GROUP):
        totals = [None] * GROUP
        for q in range(quants):
            for d in range(3):
                block = stiffened[d * basis:(d + 1) * basis, q * lanes:(q + 1) * lanes]
                for i in range(GROUP):
                    term = block * jac[q, start + i, d:d + 1, :]
                    totals[i] = term if totals[i] is None else totals[i] + term
        take(start, totals)


def mix_faces(table, flux, side, start, quants, lanes):
    totals = [[] for _ in range(GROUP)]
    for f in range(4):
        blocks = [
            table[q * ROWS:(q + 1) * ROWS, f * lanes:(f + 1) * lanes] for q in range(quants)
        ]
        for i in range(GROUP):
            total = blocks[0] * flux[side, 0, start + i, f:f + 1, :]
            for q in range(1, quants):
                total = total + blocks[q] * flux[side, q, start + i, f:f + 1, :]
            totals[i].append(total)
    return [jnp.concatenate(total, axis=0) for total in totals]


def fill_projector(projector, padded):
    modes, faces, basis = projector.shape
    padded[...] = jnp.zeros(padded.shape, F32)
    for f in range(faces):
        for m in range(modes):
            padded[f * ROWS + m:f * ROWS + m + 1, 0:basis] = projector[m, f:f + 1, :]


def predict(stiff_fold, jac, state, stiffened, first, second, basis, quants, lanes):
    for start in range(0, quants, GROUP):
        values = [state(q) for q in range(start, start + GROUP)]
        stiffen(stiff_fold, values, stiffened.at[0], start, lanes)
    for order in range(1, ORDER):
        factor = 1.0 / math.factorial(order + 1)

        def take(start, totals):
            if order + 1 < ORDER:
                stiffen(stiff_fold, totals, stiffened.at[order % 2], start, lanes)
            for p, total in enumerate(totals, start):
                first[p] = first[p] + factor * total
                if second is not None:
                    second[p] = second[p] + (2.0 ** (order + 1) - 1.0) * factor * total

        mix_jacobians(stiffened.at[(order - 1) % 2], jac, basis, quants, lanes, take)


def dense_rows(quants, modes):
    return -(-quants * modes // 32) * 32


def project_table(padded, field, table, dense, basis, quants, lanes, modes):
    fold = fold_columns(padded[:, 0:basis])
    last = dense.shape[0]
    dense[last - 8:last] = jnp.zeros((8, dense.shape[1]), F32)
    for start in range(0, quants, GROUP):
        values = [fold_rows(field(q)) for q in range(start, start + GROUP)]
        flat = dot(fold, jnp.concatenate(values, axis=1))
        for q in range(start, start + GROUP):
            for f in range(4):
                block = flat[f * ROWS:(f + 1) * ROWS, (q - start) * lanes:(q - start + 1) * lanes]
                columns = slice(f * lanes, (f + 1) * lanes)
                table[q * ROWS:(q + 1) * ROWS, columns] = block
                dense[q * modes:(q + 1) * modes, columns] = block[0:modes]


def even_spot():
    return [lax.rem(lax.axis_index(axis), 2) == 0 for axis in ("dom", "sub")]


def send_choice(send_row, faces, lanes):
    low = jnp.broadcast_to(send_row[:, 0:lanes], (8, lanes))
    lane = iota((8, lanes), 1)
    turned = pltpu.roll(low, SLOTS_DOM, 1)
    high = send_row[:, 2 * SLOTS_DOM:2 * SLOTS_DOM + 2 * SLOTS_SUB]
    spread = jnp.broadcast_to(jnp.concatenate([high, high], axis=1), (8, lanes))
    moved = pltpu.roll(spread, SLOTS_SUB, 1)
    left = lax.rem(lane, 2 * SLOTS_SUB) < SLOTS_SUB
    pieces = [
        jnp.where(lane < SLOTS_DOM, low, turned),
        jnp.where(lane < SLOTS_DOM, turned, low),
        jnp.where(left, spread, moved),
        jnp.where(left, moved, spread),
    ]
    even_dom, even_sub = even_spot()
    pieces = [
        jnp.where(even_dom, pieces[1], pieces[0]),
        jnp.where(even_dom, pieces[0], pieces[1]),
        jnp.where(even_sub, pieces[3], pieces[2]),
        jnp.where(even_sub, pieces[2], pieces[3]),
    ]
    return one_hot(jnp.concatenate([piece[0:1] for piece in pieces], axis=1), 0, faces)


def pick_sends(dense, chosen, outs, lanes):
    sent = gather(dense[...], chosen)
    for k, count in enumerate(PACKING):
        out = outs[min(k, 2)]
        rows = sent.shape[0] // count
        values = sent[:, k * lanes:(k + 1) * lanes]
        spot = iota((rows, lanes), 1)
        packed = values[0:rows]
        for g in range(1, count):
            packed = jnp.where(
                spot >= g * (lanes // count), values[g * rows:(g + 1) * rows], packed
            )
        row = rows if k == 3 else 0
        out[row:row + rows] = packed


def spread_received(arrived, count, lanes):
    width = lanes // count
    place = iota(arrived.shape, 1)
    return jnp.concatenate(
        [
            jnp.where((place >= g * width) & (place < (g + 1) * width), arrived, 0.0)
            for g in range(count)
        ],
        axis=0,
    )


def pick_local(table, slot, faces):
    chosen = jnp.concatenate([one_hot(slot[f:f + 1], 0, faces) for f in range(4)], axis=1)
    return gather(table, chosen)


def received_choice(slot, faces, lanes):
    even_dom, even_sub = even_spot()
    starts = (
        jnp.where(even_dom, faces + SLOTS_DOM, faces),
        faces + 2 * SLOTS_DOM + jnp.where(even_sub, SLOTS_SUB, 0),
        jnp.where(even_dom, faces, faces + SLOTS_DOM),
        faces + 2 * SLOTS_DOM + jnp.where(even_sub, 0, SLOTS_SUB),
    )
    widths = (SLOTS_DOM, SLOTS_SUB, SLOTS_DOM, SLOTS_SUB)
    return jnp.concatenate(
        [
            jnp.concatenate(
                [one_hot(slot[f:f + 1], first, lanes, width) for f in range(4)], axis=1
            )
            for first, width in zip(starts, widths)
        ],
        axis=0,
    )


def add_received(picked, dom, sub, chosen, dense, quants, modes, lanes):
    pieces = zip((dom, sub), (PACKING[0], PACKING[2]))
    spread = jnp.concatenate(
        [spread_received(item, count, lanes) for item, count in pieces], axis=1
    )
    dense[...] = gather(spread, chosen)
    for q in range(quants):
        rows = slice(q * ROWS, q * ROWS + modes)
        picked[rows] = picked[rows] + dense[q * modes:(q + 1) * modes]


def add_early(picked, dom, near, chosen, dense, quants, modes, lanes):
    half = near.shape[0] // 2
    add_received(
        picked, dom[...], near[0:half], chosen[0:2 * lanes], dense, quants, modes, lanes
    )


def add_late(picked, dom, far, chosen, dense, quants, modes, lanes):
    spot, count = lax.axis_index("sub"), lax.axis_size("sub")
    met = jnp.where(lax.rem(spot, 2) == 0, spot > 0, spot < count - 1)
    piece = jnp.where(met, far[...], 0.0)
    add_received(
        picked, dom[...], piece, chosen[2 * lanes:4 * lanes], dense, quants, modes, lanes
    )


def lift_weights(lifting):
    basis, depth = lifting.shape
    rest = jnp.zeros((fold_step(basis) - basis, depth), F32)
    high, low = halves(jnp.concatenate([lifting, rest], axis=0))
    return jnp.concatenate([high, low], axis=0)


def lift(weights, high, low, basis):
    step = fold_step(basis)
    both = dot(weights, high)
    return both[0:basis] + both[step:step + basis] + dot(weights[0:step], low)[0:basis]


def local_update(
    base, integral, table, jac, turned_fold, flux, lifting, stiffened, part,
    basis, quants, lanes,
):
    for start in range(0, quants, GROUP):
        values = [integral(q) for q in range(start, start + GROUP)]
        stiffen(turned_fold, values, stiffened, start, lanes)
    weights = lift_weights(lifting)
    for start in range(0, quants, GROUP):
        solved = mix_faces(table, flux, 0, start, quants, lanes)
        high, low = halves(jnp.concatenate(solved, axis=1))
        own = lift(weights, high, low, basis)
        for i in range(GROUP):
            part[start + i] = base(start + i) - own[:, i * lanes:(i + 1) * lanes]

    def take(start, totals):
        for p, total in enumerate(totals, start):
            part[p] = part[p] + total

    mix_jacobians(stiffened, jac, basis, quants, lanes, take)


def near_lift(picked, flux, orient, lifting, quants, lanes, take):
    weights = lift_weights(lifting)
    masks = [
        jnp.concatenate(
            [
                jnp.broadcast_to(jnp.where(orient[f:f + 1] == o, 1.0, 0.0), (ROWS, lanes))
                for f in range(4)
            ],
            axis=0,
        ).astype(BF16)
        for o in range(3)
    ]
    for start in range(0, quants, GROUP):
        highs, lows = [], []
        for solved in mix_faces(picked, flux, 1, start, quants, lanes):
            high, low = halves(solved)
            highs.append(jnp.concatenate([high * mask for mask in masks], axis=0))
            lows.append(jnp.concatenate([low * mask for mask in masks], axis=0))
        near = lift(
            weights, jnp.concatenate(highs, axis=1), jnp.concatenate(lows, axis=1),
            lifting.shape[0],
        )
        for i in range(GROUP):
            take(start + i, near[:, i * lanes:(i + 1) * lanes])


def near_lifting(own_lifting, rotations):
    count, modes, _ = rotations.shape
    block = 4 * ROWS
    row, column = iota((modes, count * block), 0), iota((modes, count * block), 1)
    turned = jnp.zeros((modes, count * block), F32)
    for o in range(count):
        spot = (lax.rem(column, ROWS) == row) & (lax.div(column, block) == o)
        turned = turned + exact_dot(rotations[o], jnp.where(spot, 1.0, 0.0))
    row, column = iota((block, modes), 0), iota((block, modes), 1)
    tall = exact_dot(jnp.where(lax.rem(row, ROWS) == column, 1.0, 0.0), turned)
    row, column = iota(tall.shape, 0), iota(tall.shape, 1)
    same = lax.div(row, ROWS) == lax.div(lax.rem(column, block), ROWS)
    return exact_dot(own_lifting, jnp.where(same, tall, 0.0))


def first_kernel(*refs):
    inputs, refs = refs[:INPUTS], refs[INPUTS:]
    held, refs = refs[:INPUTS], refs[INPUTS:]
    first, second, table, padded, stiff_fold, choice, *sends, stiffened, dense, arrivals = refs
    copies = [
        pltpu.make_async_copy(source, target, arrivals.at[k])
        for k, (source, target) in enumerate(zip(inputs, held))
    ]
    for copy in copies:
        copy.start()
    send_row, projector, stiffness, state, jac = held[:FIRST_USED]
    quants, basis, lanes = state.shape
    modes = projector.shape[0]
    copies[0].wait()
    choice[...] = send_choice(send_row, 4 * lanes, lanes)
    copies[1].wait()
    fill_projector(projector, padded)
    copies[2].wait()
    fold = fold_columns(jnp.concatenate([stiffness[d] for d in range(3)], axis=0))
    stiff_fold[...] = fold.astype(F32)
    copies[3].wait()
    for q in range(quants):
        value = state[q]
        first[q] = value
        second[q] = value
    copies[4].wait()
    predict(
        fold, jac, lambda q: state[q], stiffened, first, second, basis, quants, lanes
    )
    project_table(
        padded, lambda q: first[q], table, dense, basis, quants, lanes, modes
    )
    pick_sends(dense, choice[...], sends, lanes)
    for copy in copies[FIRST_USED:]:
        copy.wait()


def second_kernel(
    state, first, table, near, dom, jac, stiffness, padded, rotations, flux, slot,
    part, picked, lifting, turned_fold, choice,
    stiffened, dense,
):
    quants, basis, lanes = state.shape
    modes = rotations.shape[1]
    turned = jnp.concatenate([stiffness[d].T for d in range(3)], axis=0)
    fold = fold_columns(turned)
    turned_fold[...] = fold.astype(F32)
    own_lifting = padded[...].T[0:basis]
    lifting[...] = near_lifting(own_lifting, rotations)
    picked[...] = pick_local(table[...], slot, 4 * lanes)
    choice[...] = received_choice(slot, 4 * lanes, lanes)
    add_early(picked, dom, near, choice, dense, quants, modes, lanes)
    local_update(
        lambda p: state[p], lambda q: first[q], table, jac, fold, flux, own_lifting,
        stiffened, part, basis, quants, lanes,
    )


def third_kernel(
    state, first, second, part, picked_early, far, dom, rotations, jac, stiff_fold, padded, flux, orient, cluster, lifting, received, choice,
    middle, integral, picked, table, *refs,
):
    *sends, stiffened, dense = refs
    quants, basis, lanes = state.shape
    modes = rotations.shape[1]
    picked[...] = picked_early[...]
    add_late(picked, dom, far, received, dense, quants, modes, lanes)
    fine = cluster[...] == 0

    def take(p, near):
        value = jnp.where(fine, part[p] - near, state[p])
        middle[p] = value
        integral[p] = value

    near_lift(picked, flux, orient, lifting[...], quants, lanes, take)
    predict(
        stiff_fold[...].astype(BF16), jac, lambda q: middle[q], stiffened, integral, None,
        basis, quants, lanes,
    )
    project_table(
        padded, lambda q: jnp.where(fine, integral[q], second[q]), table, dense,
        basis, quants, lanes, modes,
    )
    for q in range(quants):
        integral[q] = jnp.where(fine, integral[q], first[q] + second[q])
    pick_sends(dense, choice[...], sends, lanes)


def fourth_kernel(
    middle, integral, table_one, table_two, picked_one, near, dom, jac, turned_fold, padded,
    rotations, flux, slot, cluster, received,
    part, picked,
    stiffened, dense, total_table,
):
    quants, basis, lanes = middle.shape
    modes = rotations.shape[1]
    own_lifting = padded[...].T[0:basis]
    coarse = jnp.concatenate([cluster[...] != 0] * 4, axis=1)
    total_table[...] = table_two[...] + jnp.where(coarse, table_one[...], 0.0)
    picked[...] = pick_local(table_two[...], slot, 4 * lanes) + jnp.where(
        coarse, picked_one[...], 0.0
    )
    add_early(picked, dom, near, received, dense, quants, modes, lanes)
    local_update(
        lambda p: middle[p], lambda q: integral[q], total_table, jac,
        turned_fold[...].astype(BF16), flux, own_lifting,
        stiffened, part, basis, quants, lanes,
    )


def fifth_kernel(
    part, picked_early, far, dom, rotations, flux, orient, lifting, received, yield_stress,
    updated,
    picked, dense,
):
    quants, basis, lanes = part.shape
    modes = rotations.shape[1]
    picked[...] = picked_early[...]
    add_late(picked, dom, far, received, dense, quants, modes, lanes)
    stepped = [None] * quants

    def take(p, near):
        stepped[p] = part[p] - near

    near_lift(picked, flux, orient, lifting[...], quants, lanes, take)
    mean_part = (stepped[0] + stepped[1] + stepped[2]) / 3.0
    spread = [stepped[q] - mean_part for q in range(3)]
    normal = [item[0:1] for item in spread]
    shear = [stepped[q][0:1] for q in range(3, 6)]
    second_inv = 0.5 * (normal[0] ** 2 + normal[1] ** 2 + normal[2] ** 2) + (
        shear[0] ** 2 + shear[1] ** 2 + shear[2] ** 2
    )
    limit = yield_stress[...]
    scaling = limit / jnp.maximum(jnp.sqrt(second_inv), limit)
    for q in range(3):
        updated[q] = mean_part + scaling * spread[q]
    for q in range(3, 6):
        updated[q] = scaling * stepped[q]
    for q in range(6, quants):
        updated[q] = stepped[q]


def run(body, outs, scratch, *operands, space=pltpu.VMEM):
    vmem = pl.BlockSpec(memory_space=pltpu.VMEM)
    return pl.pallas_call(
        body,
        out_shape=[
            out if isinstance(out, jax.ShapeDtypeStruct) else jax.ShapeDtypeStruct(out, F32)
            for out in outs
        ],
        in_specs=[pl.BlockSpec(memory_space=space)] * len(operands),
        out_specs=[vmem] * len(outs),
        scratch_shapes=scratch,
        compiler_params=pltpu.CompilerParams(vmem_limit_bytes=32 * 1024 * 1024),
        name=body.__name__,
    )(*operands)


def hand_on(near, dom, onward):
    rows = onward.shape[0]
    onward[...] = near[rows:2 * rows]


def exchange(sends):
    def swap(value, axis, first):
        lower = range(first, lax.axis_size(axis) - 1, 2)
        return lax.ppermute(
            value, axis, [(i, i + 1) for i in lower] + [(i + 1, i) for i in lower]
        )

    count = lax.axis_size("sub")
    near = swap(sends[2], "sub", 0)
    dom_even = swap(sends[0], "dom", 0)
    kept, = run(hand_on, [(near.shape[0] // 2, near.shape[1])], [], near, dom_even)
    onward = [(i, (i + (2 if i % 2 == 0 else -2)) % count) for i in range(count)]
    far = lax.ppermute(kept, "sub", onward)
    dom_odd = swap(sends[1], "dom", 1)
    return (near, dom_even), (far, dom_odd)


def on_device(
    modal_state,
    stiffness,
    jacobians,
    flux_solvers,
    projector,
    rotations,
    yield_stress,
    cluster,
    orient,
    neighbour_slot,
    send_map,
):
    basis, quants, lanes = modal_state.shape
    inputs = [
        send_map.reshape(1, -1),
        jnp.transpose(projector, (1, 0, 2)),
        stiffness,
        jnp.transpose(modal_state, (1, 0, 2)),
        jnp.transpose(jacobians, (1, 2, 0, 3)),
        jnp.transpose(flux_solvers, (0, 2, 3, 1, 4)),
        rotations,
        neighbour_slot,
        orient,
        cluster.reshape(1, lanes),
        yield_stress.reshape(1, lanes),
    ]
    inputs = [pltpu.with_memory_space_constraint(item, pltpu.HBM) for item in inputs]
    held = [jax.ShapeDtypeStruct(item.shape, item.dtype) for item in inputs]

    field = (quants, basis, lanes)
    table = (quants * ROWS, 4 * lanes)
    rows = dense_rows(quants, projector.shape[1])
    dense = pltpu.VMEM((rows, 4 * lanes), F32)
    messages = [(rows // 2, lanes)] * 3
    choice = jax.ShapeDtypeStruct((4 * lanes, 4 * lanes), BF16)
    flat = quants * lanes
    fold = (3 * basis, 3 * fold_step(basis))
    stiffened = pltpu.VMEM((3 * basis, flat), F32)
    two_stiffened = pltpu.VMEM((2, 3 * basis, flat), F32)

    outs = run(
        first_kernel,
        held + [field, field, table, (4 * ROWS, 128), fold, choice] + messages,
        [two_stiffened, dense, pltpu.SemaphoreType.DMA((INPUTS,))],
        *inputs, space=pl.ANY,
    )
    _, _, stiff, state, jac, flux, turns, slot, orient, cluster, limit = outs[:INPUTS]
    first, second, table_one, padded, stiff_fold, sending, *sends = outs[INPUTS:]
    early, late = exchange(sends)
    part_one, local_one, lifting, turned_fold, received = run(
        second_kernel, [field, table, (basis, 3 * 4 * ROWS), fold, choice], [stiffened, dense],
        state, first, table_one, *early, jac, stiff, padded, turns, flux, slot,
    )
    middle, integral, picked_one, table_two, *sends = run(
        third_kernel, [field, field, table, table] + messages, [two_stiffened, dense],
        state, first, second, part_one, local_one, *late, turns,
        jac, stiff_fold, padded, flux, orient, cluster, lifting, received, sending,
    )
    early, late = exchange(sends)
    part_two, local_two = run(
        fourth_kernel, [field, table], [stiffened, dense, pltpu.VMEM(table, F32)],
        middle, integral, table_one, table_two, picked_one, *early, jac, turned_fold, padded,
        turns, flux, slot, cluster, received,
    )
    updated, = run(
        fifth_kernel, [field], [pltpu.VMEM(table, F32), dense],
        part_two, local_two, *late, turns, flux, orient, lifting, received, limit,
    )
    return jnp.transpose(updated, (1, 0, 2))


def solution(mesh):
    placed = (
        P(None, None, ("dom", "sub")),
        P(),
        P(None, None, None, ("dom", "sub")),
        P(None, None, None, None, ("dom", "sub")),
        P(),
        P(),
        P(("dom", "sub")),
        P(("dom", "sub")),
        P(None, ("dom", "sub")),
        P(None, ("dom", "sub")),
        P(("dom", "sub")),
    )
    return jax.shard_map(
        on_device,
        mesh=mesh,
        in_specs=placed,
        out_specs=P(None, None, ("dom", "sub")),
        check_vma=False,
    )
```

profile of v0, /device:TPU:0, one launch (start us, length us, event | category | flops | bytes accessed | tf_op | source)
XLA Modules:
  0.0 30.6 jit_solution(15337049979479535253)
XLA Ops:
  0.0 6.2 %first_kernel.1 = (s32[1,192]{1,0:T(1,128)}, f32[21,4,56]{2,1,0:T(4,128)}, f32[3,56,56]{2,1,0:T(8,128)S(1)}, f32[9,56,128]{2,1,0:T(8,128)S(1)}, f32[9,9,3,128]{3...) custom-call(s32[1,192]{1,0:T(1,128)} %bitcast.12, ...), custom_call_target="tpu_custom_call" | custom-call | tf_op jit(solution)/shard_map/first_kernel/pallas_call | solution.py:487
  6.2 3.0 %collective-permute-start = (f32[96,128]{1,0:T(8,128)S(1)}, f32[96,128]{1,0:T(8,128)S(1)}, u32[]{:S(2)}, u32[]{:S(2)}) collective-permute-start(f32[96,128]{1,0:T(8,128)S(1)} %get-tuple-element.41), channel_id=1, source_target_pairs={{0,1},{2,3},{1,0},{3,2},{4,5},{6,7},{5,4},{7,6},{8,9},{10,11},{9,8... | collective-permute-start | bytes 147464 | tf_op jit(solution)/shard_map/ppermute | solution.py:509
  9.2 0.0 collective-permute-start.1
  9.2 0.7 %collective-permute-start.3 = (f32[96,128]{1,0:T(8,128)S(1)}, f32[96,128]{1,0:T(8,128)S(1)}, u32[]{:S(2)}, u32[]{:S(2)}) collective-permute-start(f32[96,128]{1,0:T(8,128)S(1)} %get-tuple-element.51), channel_id=1, source_target_pairs={{4,8},{12,16},{20,24},{8,4},{16,12},{24,20},{5,9},{13,17},{21,25},... | collective-permute-start | bytes 147464 | tf_op jit(solution)/shard_map/ppermute | solution.py:509
  9.9 1.4 %collective-permute-done.near = f32[96,128]{1,0:T(8,128)S(1)} collective-permute-done((f32[96,128]{1,0:T(8,128)S(1)}, f32[96,128]{1,0:T(8,128)S(1)}, u32[]{:S(2)}, u32[]{:S(2)}) %collective-permute-start) | collective-permute-done | bytes 49184 | tf_op jit(solution)/shard_map/ppermute | solution.py:509
  11.3 0.0 collective-permute-done.1.dom
  11.3 2.0 %collective-permute-start.2 = (f32[48,128]{1,0:T(8,128)S(1)}, f32[48,128]{1,0:T(8,128)S(1)}, u32[]{:S(2)}, u32[]{:S(2)}) collective-permute-start(f32[48,128]{1,0:T(8,128)S(1)} %hand_on.2), channel_id=1, source_target_pairs={{0,2},{1,3},{2,0},{3,1},{4,6},{5,7},{6,4},{7,5},{8,10},{9,11},{10,... | collective-permute-start | bytes 73736 | tf_op jit(solution)/shard_map/ppermute | solution.py:518
  13.3 2.3 %second_kernel.1 = (f32[9,56,128]{2,1,0:T(8,128)S(1)}, f32[216,512]{1,0:T(8,128)S(1)}, f32[56,288]{1,0:T(8,128)S(1)}, f32[168,192]{1,0:T(8,128)S(1)}, bf16[512,512]{1,0:T(8,128)(2,1)S(1)}) custom-call(f32[9,56,128]{2,1,0:T(8,128)S(1)} %get-tuple-element.37.state, f32[9,56,128]{2,1,0:T(8,128)S(1)} %get-tuple-element.38.first, ...), custom_call_target="tpu_custom_call" | custom-call | tf_op jit(solution)/shard_map/second_kernel/pallas_call | solution.py:487
  15.6 0.0 collective-permute-done.3.dom
  15.6 0.0 collective-permute-done.2.far
  15.6 4.9 %third_kernel.1 = (f32[9,56,128]{2,1,0:T(8,128)S(1)}, f32[9,56,128]{2,1,0:T(8,128)S(1)}, f32[216,512]{1,0:T(8,128)S(1)}, f32[216,512]{1,0:T(8,128)S(1)}, f32[96,...) custom-call(f32[9,56,128]{2,1,0:T(8,128)S(1)} %get-tuple-element.37.state, ...), custom_call_target="tpu_custom_call" | custom-call | tf_op jit(solution)/shard_map/third_kernel/pallas_call | solution.py:487
  20.6 1.6 %collective-permute-start.4 = (f32[96,128]{1,0:T(8,128)S(1)}, f32[96,128]{1,0:T(8,128)S(1)}, u32[]{:S(2)}, u32[]{:S(2)}) collective-permute-start(f32[96,128]{1,0:T(8,128)S(1)} %get-tuple-element.62), channel_id=1, source_target_pairs={{0,1},{2,3},{1,0},{3,2},{4,5},{6,7},{5,4},{7,6},{8,9},{10,11},{9,8... | collective-permute-start | bytes 147464 | tf_op jit(solution)/shard_map/ppermute | solution.py:509
  22.1 0.0 collective-permute-start.5
  22.1 0.7 %collective-permute-start.7 = (f32[96,128]{1,0:T(8,128)S(1)}, f32[96,128]{1,0:T(8,128)S(1)}, u32[]{:S(2)}, u32[]{:S(2)}) collective-permute-start(f32[96,128]{1,0:T(8,128)S(1)} %get-tuple-element.67), channel_id=1, source_target_pairs={{4,8},{12,16},{20,24},{8,4},{16,12},{24,20},{5,9},{13,17},{21,25},... | collective-permute-start | bytes 147464 | tf_op jit(solution)/shard_map/ppermute | solution.py:509
  22.8 2.3 %collective-permute-done.4.near = f32[96,128]{1,0:T(8,128)S(1)} collective-permute-done((f32[96,128]{1,0:T(8,128)S(1)}, f32[96,128]{1,0:T(8,128)S(1)}, u32[]{:S(2)}, u32[]{:S(2)}) %collective-permute-start.4) | collective-permute-done | bytes 49184 | tf_op jit(solution)/shard_map/ppermute | solution.py:509
  25.1 0.0 collective-permute-done.5.dom
  25.1 1.3 %collective-permute-start.6 = (f32[48,128]{1,0:T(8,128)S(1)}, f32[48,128]{1,0:T(8,128)S(1)}, u32[]{:S(2)}, u32[]{:S(2)}) collective-permute-start(f32[48,128]{1,0:T(8,128)S(1)} %hand_on.3), channel_id=1, source_target_pairs={{0,2},{1,3},{2,0},{3,1},{4,6},{5,7},{6,4},{7,5},{8,10},{9,11},{10,... | collective-permute-start | bytes 73736 | tf_op jit(solution)/shard_map/ppermute | solution.py:518
  26.4 1.6 %fourth_kernel.1 = (f32[9,56,128]{2,1,0:T(8,128)S(1)}, f32[216,512]{1,0:T(8,128)S(1)}) custom-call(f32[9,56,128]{2,1,0:T(8,128)S(1)} %get-tuple-element.58.middle, f32[9,56,128]{2,1,0:T(8,128)S(1)} %get-tuple-element.59.integral, f32[216,512]{1,0:T(8,128)S(1)} %get-tuple-element.40.table.table_one, f32[216,512]{1,0:T(8,128)S(1)} %get-tuple-element.60.table_two, ...), custom_call_target="tpu_custom_call" | custom-call | tf_op jit(solution)/shard_map/fourth_kernel/pallas_call | solution.py:487
  27.9 0.0 collective-permute-done.7.dom
  28.0 1.0 %collective-permute-done.6.far = f32[48,128]{1,0:T(8,128)S(1)} collective-permute-done((f32[48,128]{1,0:T(8,128)S(1)}, f32[48,128]{1,0:T(8,128)S(1)}, u32[]{:S(2)}, u32[]{:S(2)}) %collective-permute-start.6) | collective-permute-done | bytes 24608 | tf_op jit(solution)/shard_map/ppermute | solution.py:518
  29.0 1.7 %fifth_kernel.1 = f32[9,56,128]{2,1,0:T(8,128)} custom-call(f32[9,56,128]{2,1,0:T(8,128)S(1)} %get-tuple-element.65.part, f32[216,512]{1,0:T(8,128)S(1)} %get-tuple-element.66.picked_early, f32[48,128]{1,0:T(8,128)S(1)} %collective-permute-done.6.far, f32[96,128]{1,0:T(8,128)S(1)} %collective-permute-done.7.dom, ...), custom_call_target="tpu_custom_call" | custom-call | tf_op jit(solution)/shard_map/fifth_kernel/pallas_call | solution.py:487
  (2 shorter events, 0.0 us)
Async XLA Ops:
  6.2 5.1 %collective-permute-start = (f32[96,128]{1,0:T(8,128)S(1)}, f32[96,128]{1,0:T(8,128)S(1)}, u32[]{:S(2)}, u32[]{:S(2)}) collective-permute-start(f32[96,128]{1,0:T(8,128)S(1)} %get-tuple-element.41), channel_id=1, source_target_pairs={{0,1},{2,3},{1,0},{3,2},{4,5},{6,7},{5,4},{7,6},{8,9},{10,11},{9,8... | collective-permute-start | bytes 147464 | tf_op jit(solution)/shard_map/ppermute | solution.py:509
  9.2 2.1 %collective-permute-start.1 = (f32[96,128]{1,0:T(8,128)S(1)}, f32[96,128]{1,0:T(8,128)S(1)}, u32[]{:S(2)}, u32[]{:S(2)}) collective-permute-start(f32[96,128]{1,0:T(8,128)S(1)} %get-tuple-element.42), channel_id=1, source_target_pairs={{0,4},{8,12},{16,20},{24,28},{4,0},{12,8},{20,16},{28,24},{1,5},{9... | collective-permute-start | bytes 147464 | tf_op jit(solution)/shard_map/ppermute | solution.py:509
  9.2 6.4 %collective-permute-start.3 = (f32[96,128]{1,0:T(8,128)S(1)}, f32[96,128]{1,0:T(8,128)S(1)}, u32[]{:S(2)}, u32[]{:S(2)}) collective-permute-start(f32[96,128]{1,0:T(8,128)S(1)} %get-tuple-element.51), channel_id=1, source_target_pairs={{4,8},{12,16},{20,24},{8,4},{16,12},{24,20},{5,9},{13,17},{21,25},... | collective-permute-start | bytes 147464 | tf_op jit(solution)/shard_map/ppermute | solution.py:509
  11.3 4.4 %collective-permute-start.2 = (f32[48,128]{1,0:T(8,128)S(1)}, f32[48,128]{1,0:T(8,128)S(1)}, u32[]{:S(2)}, u32[]{:S(2)}) collective-permute-start(f32[48,128]{1,0:T(8,128)S(1)} %hand_on.2), channel_id=1, source_target_pairs={{0,2},{1,3},{2,0},{3,1},{4,6},{5,7},{6,4},{7,5},{8,10},{9,11},{10,... | collective-permute-start | bytes 73736 | tf_op jit(solution)/shard_map/ppermute | solution.py:518
  20.6 4.5 %collective-permute-start.4 = (f32[96,128]{1,0:T(8,128)S(1)}, f32[96,128]{1,0:T(8,128)S(1)}, u32[]{:S(2)}, u32[]{:S(2)}) collective-permute-start(f32[96,128]{1,0:T(8,128)S(1)} %get-tuple-element.62), channel_id=1, source_target_pairs={{0,1},{2,3},{1,0},{3,2},{4,5},{6,7},{5,4},{7,6},{8,9},{10,11},{9,8... | collective-permute-start | bytes 147464 | tf_op jit(solution)/shard_map/ppermute | solution.py:509
  22.1 3.0 %collective-permute-start.5 = (f32[96,128]{1,0:T(8,128)S(1)}, f32[96,128]{1,0:T(8,128)S(1)}, u32[]{:S(2)}, u32[]{:S(2)}) collective-permute-start(f32[96,128]{1,0:T(8,128)S(1)} %get-tuple-element.63), channel_id=1, source_target_pairs={{0,4},{8,12},{16,20},{24,28},{4,0},{12,8},{20,16},{28,24},{1,5},{9... | collective-permute-start | bytes 147464 | tf_op jit(solution)/shard_map/ppermute | solution.py:509
  22.1 5.8 %collective-permute-start.7 = (f32[96,128]{1,0:T(8,128)S(1)}, f32[96,128]{1,0:T(8,128)S(1)}, u32[]{:S(2)}, u32[]{:S(2)}) collective-permute-start(f32[96,128]{1,0:T(8,128)S(1)} %get-tuple-element.67), channel_id=1, source_target_pairs={{4,8},{12,16},{20,24},{8,4},{16,12},{24,20},{5,9},{13,17},{21,25},... | collective-permute-start | bytes 147464 | tf_op jit(solution)/shard_map/ppermute | solution.py:509
  25.1 3.9 %collective-permute-start.6 = (f32[48,128]{1,0:T(8,128)S(1)}, f32[48,128]{1,0:T(8,128)S(1)}, u32[]{:S(2)}, u32[]{:S(2)}) collective-permute-start(f32[48,128]{1,0:T(8,128)S(1)} %hand_on.3), channel_id=1, source_target_pairs={{0,2},{1,3},{2,0},{3,1},{4,6},{5,7},{6,4},{7,5},{8,10},{9,11},{10,... | collective-permute-start | bytes 73736 | tf_op jit(solution)/shard_map/ppermute | solution.py:518
where the time goes:
time: 30.8 us; the launch traced here: 30.6 us
  Pallas kernels  16.7 us (54%)
  starting transfers between devices  9.19 us (30%)
  waiting for transfers between devices  4.72 us (15%)
    pallas_call x7, Pallas kernels, run(): pl.pallas_call(body, out_shape=[out if isinstance(out, jax.ShapeDtypeStru...  16.7 us
    ppermute x6, starting transfers between devices, swap(): lax.ppermute(value, axis, [(i, i + 1) for i in lower] + [(i + 1, i) for i...  5.88 us
    ppermute x6, waiting for transfers between devices, swap(): lax.ppermute(value, axis, [(i, i + 1) for i in lower] + [(i + 1, i) for i...  3.72 us
    ppermute x2, starting transfers between devices, exchange(): far = lax.ppermute(kept, 'sub', onward)  3.31 us
    ppermute x2, waiting for transfers between devices, exchange(): far = lax.ppermute(kept, 'sub', onward)  1.01 us
  transfers between devices with their start and end apart: 8, of which 3 were waited for; matrix products, arithmetic and copies ran while one was open for 0% of the time, Pallas kernels for 13%

commit v1 on v0

--- a/solution.py
+++ b/solution.py
@@ -91,10 +91,11 @@
         for q in range(quants):
             for d in range(3):
                 block = stiffened[d * basis:(d + 1) * basis, q * lanes:(q + 1) * lanes]
+                block = block.reshape(basis // 8, 8, lanes)
                 for i in range(GROUP):
-                    term = block * jac[q, start + i, d:d + 1, :]
+                    term = block * jac[(q * quants + start + i) * 3 + d]
                     totals[i] = term if totals[i] is None else totals[i] + term
-        take(start, totals)
+        take(start, [total.reshape(basis, lanes) for total in totals])
 
 
 def mix_faces(table, flux, side, start, quants, lanes):
@@ -343,14 +344,14 @@
 def first_kernel(*refs):
     inputs, refs = refs[:INPUTS], refs[INPUTS:]
     held, refs = refs[:INPUTS], refs[INPUTS:]
-    first, second, table, padded, stiff_fold, choice, *sends, stiffened, dense, arrivals = refs
+    first, second, table, padded, stiff_fold, choice, jac, *sends, stiffened, dense, arrivals = refs
     copies = [
         pltpu.make_async_copy(source, target, arrivals.at[k])
         for k, (source, target) in enumerate(zip(inputs, held))
     ]
     for copy in copies:
         copy.start()
-    send_row, projector, stiffness, state, jac = held[:FIRST_USED]
+    send_row, projector, stiffness, state, rows = held[:FIRST_USED]
     quants, basis, lanes = state.shape
     modes = projector.shape[0]
     copies[0].wait()
@@ -366,6 +367,12 @@
         first[q] = value
         second[q] = value
     copies[4].wait()
+    for q in range(quants):
+        for p in range(quants):
+            for d in range(3):
+                jac[(q * quants + p) * 3 + d] = jnp.broadcast_to(
+                    rows[q, p, d:d + 1, :], (8, lanes)
+                )
     predict(
         fold, jac, lambda q: state[q], stiffened, first, second, basis, quants, lanes
     )
@@ -563,12 +570,12 @@
 
     outs = run(
         first_kernel,
-        held + [field, field, table, (4 * ROWS, 128), fold, choice] + messages,
+        held + [field, field, table, (4 * ROWS, 128), fold, choice, (3 * quants * quants, 8, lanes)] + messages,
         [two_stiffened, dense, pltpu.SemaphoreType.DMA((INPUTS,))],
         *inputs, space=pl.ANY,
     )
-    _, _, stiff, state, jac, flux, turns, slot, orient, cluster, limit = outs[:INPUTS]
-    first, second, table_one, padded, stiff_fold, sending, *sends = outs[INPUTS:]
+    _, _, stiff, state, _, flux, turns, slot, orient, cluster, limit = outs[:INPUTS]
+    first, second, table_one, padded, stiff_fold, sending, jac, *sends = outs[INPUTS:]
     early, late = exchange(sends)
     part_one, local_one, lifting, turned_fold, received = run(
         second_kernel, [field, table, (basis, 3 * 4 * ROWS), fold, choice], [stiffened, dense],

time: 30.8 us -> 31.3 us (1.016)
  Pallas kernels: 16.7 us -> 17.2 us
    pallas_call x7, Pallas kernels: 16.7 us -> 17.2 us  [run(): pl.pallas_call(body, out_shape=[out if isinstance(out, jax.ShapeDtypeStru...]
where the time goes in v1:
time: 31.3 us; the launch traced here: 31.1 us
  Pallas kernels  17.2 us (55%)
  starting transfers between devices  9.16 us (29%)
  waiting for transfers between devices  4.68 us (15%)
    pallas_call x7, Pallas kernels, run(): pl.pallas_call(body, out_shape=[out if isinstance(out, jax.ShapeDtypeStru...  17.2 us
    ppermute x6, starting transfers between devices, swap(): lax.ppermute(value, axis, [(i, i + 1) for i in lower] + [(i + 1, i) for i...  5.87 us
    ppermute x6, waiting for transfers between devices, swap(): lax.ppermute(value, axis, [(i, i + 1) for i in lower] + [(i + 1, i) for i...  3.72 us
    ppermute x2, starting transfers between devices, exchange(): far = lax.ppermute(kept, 'sub', onward)  3.3 us
    ppermute x2, waiting for transfers between devices, exchange(): far = lax.ppermute(kept, 'sub', onward)  0.96 us
  transfers between devices with their start and end apart: 8, of which 3 were waited for; matrix products, arithmetic and copies ran while one was open for 0% of the time, Pallas kernels for 13%

profile of v1, /device:TPU:0, one launch (start us, length us, event | category | flops | bytes accessed | tf_op | source)
XLA Modules:
  0.0 31.1 jit_solution(14773104542134503020)
XLA Ops:
  0.0 6.4 %first_kernel.1 = (s32[1,192]{1,0:T(1,128)}, f32[21,4,56]{2,1,0:T(4,128)}, f32[3,56,56]{2,1,0:T(8,128)S(1)}, f32[9,56,128]{2,1,0:T(8,128)S(1)}, f32[9,9,3,128]{3...) custom-call(s32[1,192]{1,0:T(1,128)} %bitcast.12, ...), custom_call_target="tpu_custom_call" | custom-call | tf_op jit(solution)/shard_map/first_kernel/pallas_call | solution.py:494
  6.4 3.0 %collective-permute-start = (f32[96,128]{1,0:T(8,128)S(1)}, f32[96,128]{1,0:T(8,128)S(1)}, u32[]{:S(2)}, u32[]{:S(2)}) collective-permute-start(f32[96,128]{1,0:T(8,128)S(1)} %get-tuple-element.41), channel_id=1, source_target_pairs={{0,1},{2,3},{1,0},{3,2},{4,5},{6,7},{5,4},{7,6},{8,9},{10,11},{9,8... | collective-permute-start | bytes 147464 | tf_op jit(solution)/shard_map/ppermute | solution.py:516
  9.4 0.0 collective-permute-start.1
  9.4 0.7 %collective-permute-start.3 = (f32[96,128]{1,0:T(8,128)S(1)}, f32[96,128]{1,0:T(8,128)S(1)}, u32[]{:S(2)}, u32[]{:S(2)}) collective-permute-start(f32[96,128]{1,0:T(8,128)S(1)} %get-tuple-element.51), channel_id=1, source_target_pairs={{4,8},{12,16},{20,24},{8,4},{16,12},{24,20},{5,9},{13,17},{21,25},... | collective-permute-start | bytes 147464 | tf_op jit(solution)/shard_map/ppermute | solution.py:516
  10.1 1.4 %collective-permute-done.near = f32[96,128]{1,0:T(8,128)S(1)} collective-permute-done((f32[96,128]{1,0:T(8,128)S(1)}, f32[96,128]{1,0:T(8,128)S(1)}, u32[]{:S(2)}, u32[]{:S(2)}) %collective-permute-start) | collective-permute-done | bytes 49184 | tf_op jit(solution)/shard_map/ppermute | solution.py:516
  11.5 0.0 collective-permute-done.1.dom
  11.5 2.1 %collective-permute-start.2 = (f32[48,128]{1,0:T(8,128)S(1)}, f32[48,128]{1,0:T(8,128)S(1)}, u32[]{:S(2)}, u32[]{:S(2)}) collective-permute-start(f32[48,128]{1,0:T(8,128)S(1)} %hand_on.2), channel_id=1, source_target_pairs={{0,2},{1,3},{2,0},{3,1},{4,6},{5,7},{6,4},{7,5},{8,10},{9,11},{10,... | collective-permute-start | bytes 73736 | tf_op jit(solution)/shard_map/ppermute | solution.py:525
  13.6 2.3 %second_kernel.1 = (f32[9,56,128]{2,1,0:T(8,128)S(1)}, f32[216,512]{1,0:T(8,128)S(1)}, f32[56,288]{1,0:T(8,128)S(1)}, f32[168,192]{1,0:T(8,128)S(1)}, bf16[512,512]{1,0:T(8,128)(2,1)S(1)}) custom-call(f32[9,56,128]{2,1,0:T(8,128)S(1)} %get-tuple-element.37.state, f32[9,56,128]{2,1,0:T(8,128)S(1)} %get-tuple-element.38.first, ...), custom_call_target="tpu_custom_call" | custom-call | tf_op jit(solution)/shard_map/second_kernel/pallas_call | solution.py:494
  15.9 0.0 collective-permute-done.3.dom
  15.9 0.0 collective-permute-done.2.far
  15.9 5.1 %third_kernel.1 = (f32[9,56,128]{2,1,0:T(8,128)S(1)}, f32[9,56,128]{2,1,0:T(8,128)S(1)}, f32[216,512]{1,0:T(8,128)S(1)}, f32[216,512]{1,0:T(8,128)S(1)}, f32[96,...) custom-call(f32[9,56,128]{2,1,0:T(8,128)S(1)} %get-tuple-element.37.state, ...), custom_call_target="tpu_custom_call" | custom-call | tf_op jit(solution)/shard_map/third_kernel/pallas_call | solution.py:494
  21.0 1.6 %collective-permute-start.4 = (f32[96,128]{1,0:T(8,128)S(1)}, f32[96,128]{1,0:T(8,128)S(1)}, u32[]{:S(2)}, u32[]{:S(2)}) collective-permute-start(f32[96,128]{1,0:T(8,128)S(1)} %get-tuple-element.62), channel_id=1, source_target_pairs={{0,1},{2,3},{1,0},{3,2},{4,5},{6,7},{5,4},{7,6},{8,9},{10,11},{9,8... | collective-permute-start | bytes 147464 | tf_op jit(solution)/shard_map/ppermute | solution.py:516
  22.5 0.0 collective-permute-start.5
  22.5 0.7 %collective-permute-start.7 = (f32[96,128]{1,0:T(8,128)S(1)}, f32[96,128]{1,0:T(8,128)S(1)}, u32[]{:S(2)}, u32[]{:S(2)}) collective-permute-start(f32[96,128]{1,0:T(8,128)S(1)} %get-tuple-element.67), channel_id=1, source_target_pairs={{4,8},{12,16},{20,24},{8,4},{16,12},{24,20},{5,9},{13,17},{21,25},... | collective-permute-start | bytes 147464 | tf_op jit(solution)/shard_map/ppermute | solution.py:516
  23.2 2.3 %collective-permute-done.4.near = f32[96,128]{1,0:T(8,128)S(1)} collective-permute-done((f32[96,128]{1,0:T(8,128)S(1)}, f32[96,128]{1,0:T(8,128)S(1)}, u32[]{:S(2)}, u32[]{:S(2)}) %collective-permute-start.4) | collective-permute-done | bytes 49184 | tf_op jit(solution)/shard_map/ppermute | solution.py:516
  25.5 0.0 collective-permute-done.5.dom
  25.5 1.2 %collective-permute-start.6 = (f32[48,128]{1,0:T(8,128)S(1)}, f32[48,128]{1,0:T(8,128)S(1)}, u32[]{:S(2)}, u32[]{:S(2)}) collective-permute-start(f32[48,128]{1,0:T(8,128)S(1)} %hand_on.3), channel_id=1, source_target_pairs={{0,2},{1,3},{2,0},{3,1},{4,6},{5,7},{6,4},{7,5},{8,10},{9,11},{10,... | collective-permute-start | bytes 73736 | tf_op jit(solution)/shard_map/ppermute | solution.py:525
  26.8 1.6 %fourth_kernel.1 = (f32[9,56,128]{2,1,0:T(8,128)S(1)}, f32[216,512]{1,0:T(8,128)S(1)}) custom-call(f32[9,56,128]{2,1,0:T(8,128)S(1)} %get-tuple-element.58.middle, f32[9,56,128]{2,1,0:T(8,128)S(1)} %get-tuple-element.59.integral, f32[216,512]{1,0:T(8,128)S(1)} %get-tuple-element.40.table.table_one, f32[216,512]{1,0:T(8,128)S(1)} %get-tuple-element.60.table_two, ...), custom_call_target="tpu_custom_call" | custom-call | tf_op jit(solution)/shard_map/fourth_kernel/pallas_call | solution.py:494
  28.4 0.0 collective-permute-done.7.dom
  28.4 1.0 %collective-permute-done.6.far = f32[48,128]{1,0:T(8,128)S(1)} collective-permute-done((f32[48,128]{1,0:T(8,128)S(1)}, f32[48,128]{1,0:T(8,128)S(1)}, u32[]{:S(2)}, u32[]{:S(2)}) %collective-permute-start.6) | collective-permute-done | bytes 24608 | tf_op jit(solution)/shard_map/ppermute | solution.py:525
  29.4 1.7 %fifth_kernel.1 = f32[9,56,128]{2,1,0:T(8,128)} custom-call(f32[9,56,128]{2,1,0:T(8,128)S(1)} %get-tuple-element.65.part, f32[216,512]{1,0:T(8,128)S(1)} %get-tuple-element.66.picked_early, f32[48,128]{1,0:T(8,128)S(1)} %collective-permute-done.6.far, f32[96,128]{1,0:T(8,128)S(1)} %collective-permute-done.7.dom, ...), custom_call_target="tpu_custom_call" | custom-call | tf_op jit(solution)/shard_map/fifth_kernel/pallas_call | solution.py:494
  (2 shorter events, 0.0 us)
Async XLA Ops:
  6.4 5.1 %collective-permute-start = (f32[96,128]{1,0:T(8,128)S(1)}, f32[96,128]{1,0:T(8,128)S(1)}, u32[]{:S(2)}, u32[]{:S(2)}) collective-permute-start(f32[96,128]{1,0:T(8,128)S(1)} %get-tuple-element.41), channel_id=1, source_target_pairs={{0,1},{2,3},{1,0},{3,2},{4,5},{6,7},{5,4},{7,6},{8,9},{10,11},{9,8... | collective-permute-start | bytes 147464 | tf_op jit(solution)/shard_map/ppermute | solution.py:516
  9.4 2.1 %collective-permute-start.1 = (f32[96,128]{1,0:T(8,128)S(1)}, f32[96,128]{1,0:T(8,128)S(1)}, u32[]{:S(2)}, u32[]{:S(2)}) collective-permute-start(f32[96,128]{1,0:T(8,128)S(1)} %get-tuple-element.42), channel_id=1, source_target_pairs={{0,4},{8,12},{16,20},{24,28},{4,0},{12,8},{20,16},{28,24},{1,5},{9... | collective-permute-start | bytes 147464 | tf_op jit(solution)/shard_map/ppermute | solution.py:516
  9.4 6.5 %collective-permute-start.3 = (f32[96,128]{1,0:T(8,128)S(1)}, f32[96,128]{1,0:T(8,128)S(1)}, u32[]{:S(2)}, u32[]{:S(2)}) collective-permute-start(f32[96,128]{1,0:T(8,128)S(1)} %get-tuple-element.51), channel_id=1, source_target_pairs={{4,8},{12,16},{20,24},{8,4},{16,12},{24,20},{5,9},{13,17},{21,25},... | collective-permute-start | bytes 147464 | tf_op jit(solution)/shard_map/ppermute | solution.py:516
  11.5 4.4 %collective-permute-start.2 = (f32[48,128]{1,0:T(8,128)S(1)}, f32[48,128]{1,0:T(8,128)S(1)}, u32[]{:S(2)}, u32[]{:S(2)}) collective-permute-start(f32[48,128]{1,0:T(8,128)S(1)} %hand_on.2), channel_id=1, source_target_pairs={{0,2},{1,3},{2,0},{3,1},{4,6},{5,7},{6,4},{7,5},{8,10},{9,11},{10,... | collective-permute-start | bytes 73736 | tf_op jit(solution)/shard_map/ppermute | solution.py:525
  21.0 4.5 %collective-permute-start.4 = (f32[96,128]{1,0:T(8,128)S(1)}, f32[96,128]{1,0:T(8,128)S(1)}, u32[]{:S(2)}, u32[]{:S(2)}) collective-permute-start(f32[96,128]{1,0:T(8,128)S(1)} %get-tuple-element.62), channel_id=1, source_target_pairs={{0,1},{2,3},{1,0},{3,2},{4,5},{6,7},{5,4},{7,6},{8,9},{10,11},{9,8... | collective-permute-start | bytes 147464 | tf_op jit(solution)/shard_map/ppermute | solution.py:516
  22.5 3.0 %collective-permute-start.5 = (f32[96,128]{1,0:T(8,128)S(1)}, f32[96,128]{1,0:T(8,128)S(1)}, u32[]{:S(2)}, u32[]{:S(2)}) collective-permute-start(f32[96,128]{1,0:T(8,128)S(1)} %get-tuple-element.63), channel_id=1, source_target_pairs={{0,4},{8,12},{16,20},{24,28},{4,0},{12,8},{20,16},{28,24},{1,5},{9... | collective-permute-start | bytes 147464 | tf_op jit(solution)/shard_map/ppermute | solution.py:516
  22.5 5.8 %collective-permute-start.7 = (f32[96,128]{1,0:T(8,128)S(1)}, f32[96,128]{1,0:T(8,128)S(1)}, u32[]{:S(2)}, u32[]{:S(2)}) collective-permute-start(f32[96,128]{1,0:T(8,128)S(1)} %get-tuple-element.67), channel_id=1, source_target_pairs={{4,8},{12,16},{20,24},{8,4},{16,12},{24,20},{5,9},{13,17},{21,25},... | collective-permute-start | bytes 147464 | tf_op jit(solution)/shard_map/ppermute | solution.py:516
  25.5 3.8 %collective-permute-start.6 = (f32[48,128]{1,0:T(8,128)S(1)}, f32[48,128]{1,0:T(8,128)S(1)}, u32[]{:S(2)}, u32[]{:S(2)}) collective-permute-start(f32[48,128]{1,0:T(8,128)S(1)} %hand_on.3), channel_id=1, source_target_pairs={{0,2},{1,3},{2,0},{3,1},{4,6},{5,7},{6,4},{7,5},{8,10},{9,11},{10,... | collective-permute-start | bytes 73736 | tf_op jit(solution)/shard_map/ppermute | solution.py:525

commit v2 on v0

--- a/solution.py
+++ b/solution.py
@@ -378,7 +378,7 @@
 
 
 def second_kernel(
-    state, first, table, near, dom, jac, stiffness, padded, rotations, flux, slot,
+    state, first, table, dom, near, jac, stiffness, padded, rotations, flux, slot,
     part, picked, lifting, turned_fold, choice,
     stiffened, dense,
 ):
@@ -429,7 +429,7 @@
 
 
 def fourth_kernel(
-    middle, integral, table_one, table_two, picked_one, near, dom, jac, turned_fold, padded,
+    middle, integral, table_one, table_two, picked_one, dom, near, jac, turned_fold, padded,
     rotations, flux, slot, cluster, received,
     part, picked,
     stiffened, dense, total_table,
@@ -517,7 +517,7 @@
     onward = [(i, (i + (2 if i % 2 == 0 else -2)) % count) for i in range(count)]
     far = lax.ppermute(kept, "sub", onward)
     dom_odd = swap(sends[1], "dom", 1)
-    return (near, dom_even), (far, dom_odd)
+    return (dom_even, near), (far, dom_odd)
 
 
 def on_device(

time: 30.8 us -> 31.3 us (1.016)
  waiting for transfers between devices: 4.72 us -> 5.63 us
  starting transfers between devices: 9.19 us -> 8.78 us
    ppermute x6, waiting for transfers between devices: 3.72 us -> 4.33 us  [swap(): lax.ppermute(value, axis, [(i, i + 1) for i in lower] + [(i + 1, i) for i...]
    ppermute x2, starting transfers between devices: 3.31 us -> 2.75 us  [exchange(): far = lax.ppermute(kept, 'sub', onward)]
  transfers between devices with their start and end apart: 8 -> 8, of which waited for: 3 -> 3; matrix products, arithmetic and copies ran while one was open for 0% -> 0% of each run, Pallas kernels for 13% -> 12%
where the time goes in v2:
time: 31.3 us; the launch traced here: 31.2 us
  Pallas kernels  16.7 us (53%)
  starting transfers between devices  8.78 us (28%)
  waiting for transfers between devices  5.63 us (18%)
    pallas_call x7, Pallas kernels, run(): pl.pallas_call(body, out_shape=[out if isinstance(out, jax.ShapeDtypeStru...  16.7 us
    ppermute x6, starting transfers between devices, swap(): lax.ppermute(value, axis, [(i, i + 1) for i in lower] + [(i + 1, i) for i...  6.03 us
    ppermute x6, waiting for transfers between devices, swap(): lax.ppermute(value, axis, [(i, i + 1) for i in lower] + [(i + 1, i) for i...  4.33 us
    ppermute x2, starting transfers between devices, exchange(): far = lax.ppermute(kept, 'sub', onward)  2.75 us
    ppermute x2, waiting for transfers between devices, exchange(): far = lax.ppermute(kept, 'sub', onward)  1.29 us
  transfers between devices with their start and end apart: 8, of which 3 were waited for; matrix products, arithmetic and copies ran while one was open for 0% of the time, Pallas kernels for 12%

profile of v2, /device:TPU:0, one launch (start us, length us, event | category | flops | bytes accessed | tf_op | source)
XLA Modules:
  0.0 31.2 jit_solution(13771963921314338605)
XLA Ops:
  0.0 6.2 %first_kernel.1 = (s32[1,192]{1,0:T(1,128)}, f32[21,4,56]{2,1,0:T(4,128)}, f32[3,56,56]{2,1,0:T(8,128)S(1)}, f32[9,56,128]{2,1,0:T(8,128)S(1)}, f32[9,9,3,128]{3...) custom-call(s32[1,192]{1,0:T(1,128)} %bitcast.12, ...), custom_call_target="tpu_custom_call" | custom-call | tf_op jit(solution)/shard_map/first_kernel/pallas_call | solution.py:487
  6.2 0.5 %collective-permute-start = (f32[96,128]{1,0:T(8,128)S(1)}, f32[96,128]{1,0:T(8,128)S(1)}, u32[]{:S(2)}, u32[]{:S(2)}) collective-permute-start(f32[96,128]{1,0:T(8,128)S(1)} %get-tuple-element.41), channel_id=1, source_target_pairs={{0,4},{8,12},{16,20},{24,28},{4,0},{12,8},{20,16},{28,24},{1,5},{9... | collective-permute-start | bytes 147464 | tf_op jit(solution)/shard_map/ppermute | solution.py:509
  6.7 2.6 %collective-permute-start.1 = (f32[96,128]{1,0:T(8,128)S(1)}, f32[96,128]{1,0:T(8,128)S(1)}, u32[]{:S(2)}, u32[]{:S(2)}) collective-permute-start(f32[96,128]{1,0:T(8,128)S(1)} %get-tuple-element.42), channel_id=1, source_target_pairs={{0,1},{2,3},{1,0},{3,2},{4,5},{6,7},{5,4},{7,6},{8,9},{10,11},{9,8... | collective-permute-start | bytes 147464 | tf_op jit(solution)/shard_map/ppermute | solution.py:509
  9.3 0.7 %collective-permute-start.3 = (f32[96,128]{1,0:T(8,128)S(1)}, f32[96,128]{1,0:T(8,128)S(1)}, u32[]{:S(2)}, u32[]{:S(2)}) collective-permute-start(f32[96,128]{1,0:T(8,128)S(1)} %get-tuple-element.51), channel_id=1, source_target_pairs={{4,8},{12,16},{20,24},{8,4},{16,12},{24,20},{5,9},{13,17},{21,25},... | collective-permute-start | bytes 147464 | tf_op jit(solution)/shard_map/ppermute | solution.py:509
  9.9 0.0 collective-permute-done.dom
  9.9 1.7 %collective-permute-done.1.near = f32[96,128]{1,0:T(8,128)S(1)} collective-permute-done((f32[96,128]{1,0:T(8,128)S(1)}, f32[96,128]{1,0:T(8,128)S(1)}, u32[]{:S(2)}, u32[]{:S(2)}) %collective-permute-start.1) | collective-permute-done | bytes 49184 | tf_op jit(solution)/shard_map/ppermute | solution.py:509
  11.6 1.8 %collective-permute-start.2 = (f32[48,128]{1,0:T(8,128)S(1)}, f32[48,128]{1,0:T(8,128)S(1)}, u32[]{:S(2)}, u32[]{:S(2)}) collective-permute-start(f32[48,128]{1,0:T(8,128)S(1)} %hand_on.2), channel_id=1, source_target_pairs={{0,2},{1,3},{2,0},{3,1},{4,6},{5,7},{6,4},{7,5},{8,10},{9,11},{10,... | collective-permute-start | bytes 73736 | tf_op jit(solution)/shard_map/ppermute | solution.py:518
  13.4 2.3 %second_kernel.1 = (f32[9,56,128]{2,1,0:T(8,128)S(1)}, f32[216,512]{1,0:T(8,128)S(1)}, f32[56,288]{1,0:T(8,128)S(1)}, f32[168,192]{1,0:T(8,128)S(1)}, bf16[512,512]{1,0:T(8,128)(2,1)S(1)}) custom-call(f32[9,56,128]{2,1,0:T(8,128)S(1)} %get-tuple-element.37.state, f32[9,56,128]{2,1,0:T(8,128)S(1)} %get-tuple-element.38.first, ...), custom_call_target="tpu_custom_call" | custom-call | tf_op jit(solution)/shard_map/second_kernel/pallas_call | solution.py:487
  15.7 0.0 collective-permute-done.3.dom
  15.7 0.0 collective-permute-done.2.far
  15.7 4.9 %third_kernel.1 = (f32[9,56,128]{2,1,0:T(8,128)S(1)}, f32[9,56,128]{2,1,0:T(8,128)S(1)}, f32[216,512]{1,0:T(8,128)S(1)}, f32[216,512]{1,0:T(8,128)S(1)}, f32[96,...) custom-call(f32[9,56,128]{2,1,0:T(8,128)S(1)} %get-tuple-element.37.state, ...), custom_call_target="tpu_custom_call" | custom-call | tf_op jit(solution)/shard_map/third_kernel/pallas_call | solution.py:487
  20.6 0.9 %collective-permute-start.4 = (f32[96,128]{1,0:T(8,128)S(1)}, f32[96,128]{1,0:T(8,128)S(1)}, u32[]{:S(2)}, u32[]{:S(2)}) collective-permute-start(f32[96,128]{1,0:T(8,128)S(1)} %get-tuple-element.62), channel_id=1, source_target_pairs={{0,4},{8,12},{16,20},{24,28},{4,0},{12,8},{20,16},{28,24},{1,5},{9... | collective-permute-start | bytes 147464 | tf_op jit(solution)/shard_map/ppermute | solution.py:509
  21.5 0.8 %collective-permute-start.5 = (f32[96,128]{1,0:T(8,128)S(1)}, f32[96,128]{1,0:T(8,128)S(1)}, u32[]{:S(2)}, u32[]{:S(2)}) collective-permute-start(f32[96,128]{1,0:T(8,128)S(1)} %get-tuple-element.63), channel_id=1, source_target_pairs={{0,1},{2,3},{1,0},{3,2},{4,5},{6,7},{5,4},{7,6},{8,9},{10,11},{9,8... | collective-permute-start | bytes 147464 | tf_op jit(solution)/shard_map/ppermute | solution.py:509
  22.3 0.7 %collective-permute-start.7 = (f32[96,128]{1,0:T(8,128)S(1)}, f32[96,128]{1,0:T(8,128)S(1)}, u32[]{:S(2)}, u32[]{:S(2)}) collective-permute-start(f32[96,128]{1,0:T(8,128)S(1)} %get-tuple-element.67), channel_id=1, source_target_pairs={{4,8},{12,16},{20,24},{8,4},{16,12},{24,20},{5,9},{13,17},{21,25},... | collective-permute-start | bytes 147464 | tf_op jit(solution)/shard_map/ppermute | solution.py:509
  23.0 0.0 collective-permute-done.4.dom
  23.0 2.7 %collective-permute-done.5.near = f32[96,128]{1,0:T(8,128)S(1)} collective-permute-done((f32[96,128]{1,0:T(8,128)S(1)}, f32[96,128]{1,0:T(8,128)S(1)}, u32[]{:S(2)}, u32[]{:S(2)}) %collective-permute-start.5) | collective-permute-done | bytes 49184 | tf_op jit(solution)/shard_map/ppermute | solution.py:509
  25.6 1.0 %collective-permute-start.6 = (f32[48,128]{1,0:T(8,128)S(1)}, f32[48,128]{1,0:T(8,128)S(1)}, u32[]{:S(2)}, u32[]{:S(2)}) collective-permute-start(f32[48,128]{1,0:T(8,128)S(1)} %hand_on.3), channel_id=1, source_target_pairs={{0,2},{1,3},{2,0},{3,1},{4,6},{5,7},{6,4},{7,5},{8,10},{9,11},{10,... | collective-permute-start | bytes 73736 | tf_op jit(solution)/shard_map/ppermute | solution.py:518
  26.6 1.6 %fourth_kernel.1 = (f32[9,56,128]{2,1,0:T(8,128)S(1)}, f32[216,512]{1,0:T(8,128)S(1)}) custom-call(f32[9,56,128]{2,1,0:T(8,128)S(1)} %get-tuple-element.58.middle, f32[9,56,128]{2,1,0:T(8,128)S(1)} %get-tuple-element.59.integral, f32[216,512]{1,0:T(8,128)S(1)} %get-tuple-element.40.table.table_one, f32[216,512]{1,0:T(8,128)S(1)} %get-tuple-element.60.table_two, ...), custom_call_target="tpu_custom_call" | custom-call | tf_op jit(solution)/shard_map/fourth_kernel/pallas_call | solution.py:487
  28.2 0.0 collective-permute-done.7.dom
  28.2 1.3 %collective-permute-done.6.far = f32[48,128]{1,0:T(8,128)S(1)} collective-permute-done((f32[48,128]{1,0:T(8,128)S(1)}, f32[48,128]{1,0:T(8,128)S(1)}, u32[]{:S(2)}, u32[]{:S(2)}) %collective-permute-start.6) | collective-permute-done | bytes 24608 | tf_op jit(solution)/shard_map/ppermute | solution.py:518
  29.5 1.7 %fifth_kernel.1 = f32[9,56,128]{2,1,0:T(8,128)} custom-call(f32[9,56,128]{2,1,0:T(8,128)S(1)} %get-tuple-element.65.part, f32[216,512]{1,0:T(8,128)S(1)} %get-tuple-element.66.picked_early, f32[48,128]{1,0:T(8,128)S(1)} %collective-permute-done.6.far, f32[96,128]{1,0:T(8,128)S(1)} %collective-permute-done.7.dom, ...), custom_call_target="tpu_custom_call" | custom-call | tf_op jit(solution)/shard_map/fifth_kernel/pallas_call | solution.py:487
  (2 shorter events, 0.0 us)
Async XLA Ops:
  6.2 3.8 %collective-permute-start = (f32[96,128]{1,0:T(8,128)S(1)}, f32[96,128]{1,0:T(8,128)S(1)}, u32[]{:S(2)}, u32[]{:S(2)}) collective-permute-start(f32[96,128]{1,0:T(8,128)S(1)} %get-tuple-element.41), channel_id=1, source_target_pairs={{0,4},{8,12},{16,20},{24,28},{4,0},{12,8},{20,16},{28,24},{1,5},{9... | collective-permute-start | bytes 147464 | tf_op jit(solution)/shard_map/ppermute | solution.py:509
  6.7 4.9 %collective-permute-start.1 = (f32[96,128]{1,0:T(8,128)S(1)}, f32[96,128]{1,0:T(8,128)S(1)}, u32[]{:S(2)}, u32[]{:S(2)}) collective-permute-start(f32[96,128]{1,0:T(8,128)S(1)} %get-tuple-element.42), channel_id=1, source_target_pairs={{0,1},{2,3},{1,0},{3,2},{4,5},{6,7},{5,4},{7,6},{8,9},{10,11},{9,8... | collective-permute-start | bytes 147464 | tf_op jit(solution)/shard_map/ppermute | solution.py:509
  9.3 6.4 %collective-permute-start.3 = (f32[96,128]{1,0:T(8,128)S(1)}, f32[96,128]{1,0:T(8,128)S(1)}, u32[]{:S(2)}, u32[]{:S(2)}) collective-permute-start(f32[96,128]{1,0:T(8,128)S(1)} %get-tuple-element.51), channel_id=1, source_target_pairs={{4,8},{12,16},{20,24},{8,4},{16,12},{24,20},{5,9},{13,17},{21,25},... | collective-permute-start | bytes 147464 | tf_op jit(solution)/shard_map/ppermute | solution.py:509
  11.6 4.1 %collective-permute-start.2 = (f32[48,128]{1,0:T(8,128)S(1)}, f32[48,128]{1,0:T(8,128)S(1)}, u32[]{:S(2)}, u32[]{:S(2)}) collective-permute-start(f32[48,128]{1,0:T(8,128)S(1)} %hand_on.2), channel_id=1, source_target_pairs={{0,2},{1,3},{2,0},{3,1},{4,6},{5,7},{6,4},{7,5},{8,10},{9,11},{10,... | collective-permute-start | bytes 73736 | tf_op jit(solution)/shard_map/ppermute | solution.py:518
  20.6 2.3 %collective-permute-start.4 = (f32[96,128]{1,0:T(8,128)S(1)}, f32[96,128]{1,0:T(8,128)S(1)}, u32[]{:S(2)}, u32[]{:S(2)}) collective-permute-start(f32[96,128]{1,0:T(8,128)S(1)} %get-tuple-element.62), channel_id=1, source_target_pairs={{0,4},{8,12},{16,20},{24,28},{4,0},{12,8},{20,16},{28,24},{1,5},{9... | collective-permute-start | bytes 147464 | tf_op jit(solution)/shard_map/ppermute | solution.py:509
  21.5 4.1 %collective-permute-start.5 = (f32[96,128]{1,0:T(8,128)S(1)}, f32[96,128]{1,0:T(8,128)S(1)}, u32[]{:S(2)}, u32[]{:S(2)}) collective-permute-start(f32[96,128]{1,0:T(8,128)S(1)} %get-tuple-element.63), channel_id=1, source_target_pairs={{0,1},{2,3},{1,0},{3,2},{4,5},{6,7},{5,4},{7,6},{8,9},{10,11},{9,8... | collective-permute-start | bytes 147464 | tf_op jit(solution)/shard_map/ppermute | solution.py:509
  22.3 5.9 %collective-permute-start.7 = (f32[96,128]{1,0:T(8,128)S(1)}, f32[96,128]{1,0:T(8,128)S(1)}, u32[]{:S(2)}, u32[]{:S(2)}) collective-permute-start(f32[96,128]{1,0:T(8,128)S(1)} %get-tuple-element.67), channel_id=1, source_target_pairs={{4,8},{12,16},{20,24},{8,4},{16,12},{24,20},{5,9},{13,17},{21,25},... | collective-permute-start | bytes 147464 | tf_op jit(solution)/shard_map/ppermute | solution.py:509
  25.6 3.8 %collective-permute-start.6 = (f32[48,128]{1,0:T(8,128)S(1)}, f32[48,128]{1,0:T(8,128)S(1)}, u32[]{:S(2)}, u32[]{:S(2)}) collective-permute-start(f32[48,128]{1,0:T(8,128)S(1)} %hand_on.3), channel_id=1, source_target_pairs={{0,2},{1,3},{2,0},{3,1},{4,6},{5,7},{6,4},{7,5},{8,10},{9,11},{10,... | collective-permute-start | bytes 73736 | tf_op jit(solution)/shard_map/ppermute | solution.py:518

commit v3 on v0

--- a/solution.py
+++ b/solution.py
@@ -130,9 +130,11 @@
             if order + 1 < ORDER:
                 stiffen(stiff_fold, totals, stiffened.at[order % 2], start, lanes)
             for p, total in enumerate(totals, start):
-                first[p] = first[p] + factor * total
+                before = state(p) if order == 1 else first[p]
+                first[p] = before + factor * total
                 if second is not None:
-                    second[p] = second[p] + (2.0 ** (order + 1) - 1.0) * factor * total
+                    before = state(p) if order == 1 else second[p]
+                    second[p] = before + (2.0 ** (order + 1) - 1.0) * factor * total
 
         mix_jacobians(stiffened.at[(order - 1) % 2], jac, basis, quants, lanes, take)
 
@@ -361,10 +363,6 @@
     fold = fold_columns(jnp.concatenate([stiffness[d] for d in range(3)], axis=0))
     stiff_fold[...] = fold.astype(F32)
     copies[3].wait()
-    for q in range(quants):
-        value = state[q]
-        first[q] = value
-        second[q] = value
     copies[4].wait()
     predict(
         fold, jac, lambda q: state[q], stiffened, first, second, basis, quants, lanes
@@ -410,9 +408,7 @@
     fine = cluster[...] == 0
 
     def take(p, near):
-        value = jnp.where(fine, part[p] - near, state[p])
-        middle[p] = value
-        integral[p] = value
+        middle[p] = jnp.where(fine, part[p] - near, state[p])
 
     near_lift(picked, flux, orient, lifting[...], quants, lanes, take)
     predict(

time: 30.8 us -> 30.8 us (level)
  no operation moved by 1% of the time
where the time goes in v3:
time: 30.8 us; the launch traced here: 30.6 us
  Pallas kernels  16.6 us (54%)
  starting transfers between devices  9.2 us (30%)
  waiting for transfers between devices  4.71 us (15%)
    pallas_call x7, Pallas kernels, run(): pl.pallas_call(body, out_shape=[out if isinstance(out, jax.ShapeDtypeStru...  16.6 us
    ppermute x6, starting transfers between devices, swap(): lax.ppermute(value, axis, [(i, i + 1) for i in lower] + [(i + 1, i) for i...  5.88 us
    ppermute x6, waiting for transfers between devices, swap(): lax.ppermute(value, axis, [(i, i + 1) for i in lower] + [(i + 1, i) for i...  3.72 us
    ppermute x2, starting transfers between devices, exchange(): far = lax.ppermute(kept, 'sub', onward)  3.33 us
    ppermute x2, waiting for transfers between devices, exchange(): far = lax.ppermute(kept, 'sub', onward)  0.99 us
  transfers between devices with their start and end apart: 8, of which 3 were waited for; matrix products, arithmetic and copies ran while one was open for 0% of the time, Pallas kernels for 13%

profile of v3, /device:TPU:0, one launch (start us, length us, event | category | flops | bytes accessed | tf_op | source)
XLA Modules:
  0.0 30.6 jit_solution(11036885113158870855)
XLA Ops:
  0.0 6.1 %first_kernel.1 = (s32[1,192]{1,0:T(1,128)}, f32[21,4,56]{2,1,0:T(4,128)}, f32[3,56,56]{2,1,0:T(8,128)S(1)}, f32[9,56,128]{2,1,0:T(8,128)S(1)}, f32[9,9,3,128]{3...) custom-call(s32[1,192]{1,0:T(1,128)} %bitcast.12, ...), custom_call_target="tpu_custom_call" | custom-call | tf_op jit(solution)/shard_map/first_kernel/pallas_call | solution.py:483
  6.2 3.0 %collective-permute-start = (f32[96,128]{1,0:T(8,128)S(1)}, f32[96,128]{1,0:T(8,128)S(1)}, u32[]{:S(2)}, u32[]{:S(2)}) collective-permute-start(f32[96,128]{1,0:T(8,128)S(1)} %get-tuple-element.41), channel_id=1, source_target_pairs={{0,1},{2,3},{1,0},{3,2},{4,5},{6,7},{5,4},{7,6},{8,9},{10,11},{9,8... | collective-permute-start | bytes 147464 | tf_op jit(solution)/shard_map/ppermute | solution.py:505
  9.2 0.0 collective-permute-start.1
  9.2 0.7 %collective-permute-start.3 = (f32[96,128]{1,0:T(8,128)S(1)}, f32[96,128]{1,0:T(8,128)S(1)}, u32[]{:S(2)}, u32[]{:S(2)}) collective-permute-start(f32[96,128]{1,0:T(8,128)S(1)} %get-tuple-element.51), channel_id=1, source_target_pairs={{4,8},{12,16},{20,24},{8,4},{16,12},{24,20},{5,9},{13,17},{21,25},... | collective-permute-start | bytes 147464 | tf_op jit(solution)/shard_map/ppermute | solution.py:505
  9.8 1.4 %collective-permute-done.near = f32[96,128]{1,0:T(8,128)S(1)} collective-permute-done((f32[96,128]{1,0:T(8,128)S(1)}, f32[96,128]{1,0:T(8,128)S(1)}, u32[]{:S(2)}, u32[]{:S(2)}) %collective-permute-start) | collective-permute-done | bytes 49184 | tf_op jit(solution)/shard_map/ppermute | solution.py:505
  11.2 0.0 collective-permute-done.1.dom
  11.2 2.0 %collective-permute-start.2 = (f32[48,128]{1,0:T(8,128)S(1)}, f32[48,128]{1,0:T(8,128)S(1)}, u32[]{:S(2)}, u32[]{:S(2)}) collective-permute-start(f32[48,128]{1,0:T(8,128)S(1)} %hand_on.2), channel_id=1, source_target_pairs={{0,2},{1,3},{2,0},{3,1},{4,6},{5,7},{6,4},{7,5},{8,10},{9,11},{10,... | collective-permute-start | bytes 73736 | tf_op jit(solution)/shard_map/ppermute | solution.py:514
  13.3 2.3 %second_kernel.1 = (f32[9,56,128]{2,1,0:T(8,128)S(1)}, f32[216,512]{1,0:T(8,128)S(1)}, f32[56,288]{1,0:T(8,128)S(1)}, f32[168,192]{1,0:T(8,128)S(1)}, bf16[512,512]{1,0:T(8,128)(2,1)S(1)}) custom-call(f32[9,56,128]{2,1,0:T(8,128)S(1)} %get-tuple-element.37.state, f32[9,56,128]{2,1,0:T(8,128)S(1)} %get-tuple-element.38.first, ...), custom_call_target="tpu_custom_call" | custom-call | tf_op jit(solution)/shard_map/second_kernel/pallas_call | solution.py:483
  15.6 0.0 collective-permute-done.3.dom
  15.6 0.0 collective-permute-done.2.far
  15.6 4.9 %third_kernel.1 = (f32[9,56,128]{2,1,0:T(8,128)S(1)}, f32[9,56,128]{2,1,0:T(8,128)S(1)}, f32[216,512]{1,0:T(8,128)S(1)}, f32[216,512]{1,0:T(8,128)S(1)}, f32[96,...) custom-call(f32[9,56,128]{2,1,0:T(8,128)S(1)} %get-tuple-element.37.state, ...), custom_call_target="tpu_custom_call" | custom-call | tf_op jit(solution)/shard_map/third_kernel/pallas_call | solution.py:483
  20.5 1.6 %collective-permute-start.4 = (f32[96,128]{1,0:T(8,128)S(1)}, f32[96,128]{1,0:T(8,128)S(1)}, u32[]{:S(2)}, u32[]{:S(2)}) collective-permute-start(f32[96,128]{1,0:T(8,128)S(1)} %get-tuple-element.62), channel_id=1, source_target_pairs={{0,1},{2,3},{1,0},{3,2},{4,5},{6,7},{5,4},{7,6},{8,9},{10,11},{9,8... | collective-permute-start | bytes 147464 | tf_op jit(solution)/shard_map/ppermute | solution.py:505
  22.1 0.0 collective-permute-start.5
  22.1 0.7 %collective-permute-start.7 = (f32[96,128]{1,0:T(8,128)S(1)}, f32[96,128]{1,0:T(8,128)S(1)}, u32[]{:S(2)}, u32[]{:S(2)}) collective-permute-start(f32[96,128]{1,0:T(8,128)S(1)} %get-tuple-element.67), channel_id=1, source_target_pairs={{4,8},{12,16},{20,24},{8,4},{16,12},{24,20},{5,9},{13,17},{21,25},... | collective-permute-start | bytes 147464 | tf_op jit(solution)/shard_map/ppermute | solution.py:505
  22.8 2.3 %collective-permute-done.4.near = f32[96,128]{1,0:T(8,128)S(1)} collective-permute-done((f32[96,128]{1,0:T(8,128)S(1)}, f32[96,128]{1,0:T(8,128)S(1)}, u32[]{:S(2)}, u32[]{:S(2)}) %collective-permute-start.4) | collective-permute-done | bytes 49184 | tf_op jit(solution)/shard_map/ppermute | solution.py:505
  25.1 0.0 collective-permute-done.5.dom
  25.1 1.3 %collective-permute-start.6 = (f32[48,128]{1,0:T(8,128)S(1)}, f32[48,128]{1,0:T(8,128)S(1)}, u32[]{:S(2)}, u32[]{:S(2)}) collective-permute-start(f32[48,128]{1,0:T(8,128)S(1)} %hand_on.3), channel_id=1, source_target_pairs={{0,2},{1,3},{2,0},{3,1},{4,6},{5,7},{6,4},{7,5},{8,10},{9,11},{10,... | collective-permute-start | bytes 73736 | tf_op jit(solution)/shard_map/ppermute | solution.py:514
  26.4 1.6 %fourth_kernel.1 = (f32[9,56,128]{2,1,0:T(8,128)S(1)}, f32[216,512]{1,0:T(8,128)S(1)}) custom-call(f32[9,56,128]{2,1,0:T(8,128)S(1)} %get-tuple-element.58.middle, f32[9,56,128]{2,1,0:T(8,128)S(1)} %get-tuple-element.59.integral, f32[216,512]{1,0:T(8,128)S(1)} %get-tuple-element.40.table.table_one, f32[216,512]{1,0:T(8,128)S(1)} %get-tuple-element.60.table_two, ...), custom_call_target="tpu_custom_call" | custom-call | tf_op jit(solution)/shard_map/fourth_kernel/pallas_call | solution.py:483
  27.9 0.0 collective-permute-done.7.dom
  27.9 1.0 %collective-permute-done.6.far = f32[48,128]{1,0:T(8,128)S(1)} collective-permute-done((f32[48,128]{1,0:T(8,128)S(1)}, f32[48,128]{1,0:T(8,128)S(1)}, u32[]{:S(2)}, u32[]{:S(2)}) %collective-permute-start.6) | collective-permute-done | bytes 24608 | tf_op jit(solution)/shard_map/ppermute | solution.py:514
  28.9 1.7 %fifth_kernel.1 = f32[9,56,128]{2,1,0:T(8,128)} custom-call(f32[9,56,128]{2,1,0:T(8,128)S(1)} %get-tuple-element.65.part, f32[216,512]{1,0:T(8,128)S(1)} %get-tuple-element.66.picked_early, f32[48,128]{1,0:T(8,128)S(1)} %collective-permute-done.6.far, f32[96,128]{1,0:T(8,128)S(1)} %collective-permute-done.7.dom, ...), custom_call_target="tpu_custom_call" | custom-call | tf_op jit(solution)/shard_map/fifth_kernel/pallas_call | solution.py:483
  (2 shorter events, 0.0 us)
Async XLA Ops:
  6.2 5.1 %collective-permute-start = (f32[96,128]{1,0:T(8,128)S(1)}, f32[96,128]{1,0:T(8,128)S(1)}, u32[]{:S(2)}, u32[]{:S(2)}) collective-permute-start(f32[96,128]{1,0:T(8,128)S(1)} %get-tuple-element.41), channel_id=1, source_target_pairs={{0,1},{2,3},{1,0},{3,2},{4,5},{6,7},{5,4},{7,6},{8,9},{10,11},{9,8... | collective-permute-start | bytes 147464 | tf_op jit(solution)/shard_map/ppermute | solution.py:505
  9.2 2.1 %collective-permute-start.1 = (f32[96,128]{1,0:T(8,128)S(1)}, f32[96,128]{1,0:T(8,128)S(1)}, u32[]{:S(2)}, u32[]{:S(2)}) collective-permute-start(f32[96,128]{1,0:T(8,128)S(1)} %get-tuple-element.42), channel_id=1, source_target_pairs={{0,4},{8,12},{16,20},{24,28},{4,0},{12,8},{20,16},{28,24},{1,5},{9... | collective-permute-start | bytes 147464 | tf_op jit(solution)/shard_map/ppermute | solution.py:505
  9.2 6.4 %collective-permute-start.3 = (f32[96,128]{1,0:T(8,128)S(1)}, f32[96,128]{1,0:T(8,128)S(1)}, u32[]{:S(2)}, u32[]{:S(2)}) collective-permute-start(f32[96,128]{1,0:T(8,128)S(1)} %get-tuple-element.51), channel_id=1, source_target_pairs={{4,8},{12,16},{20,24},{8,4},{16,12},{24,20},{5,9},{13,17},{21,25},... | collective-permute-start | bytes 147464 | tf_op jit(solution)/shard_map/ppermute | solution.py:505
  11.2 4.4 %collective-permute-start.2 = (f32[48,128]{1,0:T(8,128)S(1)}, f32[48,128]{1,0:T(8,128)S(1)}, u32[]{:S(2)}, u32[]{:S(2)}) collective-permute-start(f32[48,128]{1,0:T(8,128)S(1)} %hand_on.2), channel_id=1, source_target_pairs={{0,2},{1,3},{2,0},{3,1},{4,6},{5,7},{6,4},{7,5},{8,10},{9,11},{10,... | collective-permute-start | bytes 73736 | tf_op jit(solution)/shard_map/ppermute | solution.py:514
  20.5 4.5 %collective-permute-start.4 = (f32[96,128]{1,0:T(8,128)S(1)}, f32[96,128]{1,0:T(8,128)S(1)}, u32[]{:S(2)}, u32[]{:S(2)}) collective-permute-start(f32[96,128]{1,0:T(8,128)S(1)} %get-tuple-element.62), channel_id=1, source_target_pairs={{0,1},{2,3},{1,0},{3,2},{4,5},{6,7},{5,4},{7,6},{8,9},{10,11},{9,8... | collective-permute-start | bytes 147464 | tf_op jit(solution)/shard_map/ppermute | solution.py:505
  22.1 3.0 %collective-permute-start.5 = (f32[96,128]{1,0:T(8,128)S(1)}, f32[96,128]{1,0:T(8,128)S(1)}, u32[]{:S(2)}, u32[]{:S(2)}) collective-permute-start(f32[96,128]{1,0:T(8,128)S(1)} %get-tuple-element.63), channel_id=1, source_target_pairs={{0,4},{8,12},{16,20},{24,28},{4,0},{12,8},{20,16},{28,24},{1,5},{9... | collective-permute-start | bytes 147464 | tf_op jit(solution)/shard_map/ppermute | solution.py:505
  22.1 5.8 %collective-permute-start.7 = (f32[96,128]{1,0:T(8,128)S(1)}, f32[96,128]{1,0:T(8,128)S(1)}, u32[]{:S(2)}, u32[]{:S(2)}) collective-permute-start(f32[96,128]{1,0:T(8,128)S(1)} %get-tuple-element.67), channel_id=1, source_target_pairs={{4,8},{12,16},{20,24},{8,4},{16,12},{24,20},{5,9},{13,17},{21,25},... | collective-permute-start | bytes 147464 | tf_op jit(solution)/shard_map/ppermute | solution.py:505
  25.1 3.8 %collective-permute-start.6 = (f32[48,128]{1,0:T(8,128)S(1)}, f32[48,128]{1,0:T(8,128)S(1)}, u32[]{:S(2)}, u32[]{:S(2)}) collective-permute-start(f32[48,128]{1,0:T(8,128)S(1)} %hand_on.3), channel_id=1, source_target_pairs={{0,2},{1,3},{2,0},{3,1},{4,6},{5,7},{6,4},{7,5},{8,10},{9,11},{10,... | collective-permute-start | bytes 73736 | tf_op jit(solution)/shard_map/ppermute | solution.py:514
